TPU v7x, 32 devices: a whole 2x2x4 slice. The times are simulated.
32 devices in a mesh: group: 4 (over x, core), dev: 8 (over z, y).
Axes of the slice: x: 2, y: 2, z: 4, core: 2. Of those that a mesh axis runs over, the one named last changes fastest.
Arguments:
- state: float32 [5, 4, 4, 4, 8, 16, 128], P(None, None, None, None, 'group', 'dev'), may hold values from -3 to 19.25, as said below
- limit_slot: int32 [8, 16, 128], P('group', 'dev'), may hold values from -1 to 127, as said below
- wall_owner: int32 [8, 16, 2], P('group', 'dev'), may hold values from 0 to 255
Outputs:
- state_next: float32 [5, 4, 4, 4, 8, 16, 128], P(None, None, None, None, 'group', 'dev')
- wall_loads: float32 [256], P(('group', 'dev'))
Inputs may be any that keep to these rules, and one draw needn't show every extreme that they name: `state`: density lies in 0.5 to 2, each velocity component in -1.5 to 1.5 and p in 0.2 to 5 at every node. A troubled element has limit_slot = destination * 16 + slot, the destination an index of dev within the element's group and the slot below 16. The troubled elements of one device have distinct values and fill whole blocks of 16 slots per destination; one device has at most 128 troubled elements, some device of every group has exactly 128, and every device is the destination of exactly 32 troubled elements of its group.
All inputs are finite; a program needn't handle non-finite values.
Results may differ from a plain program's by a relative error of at most 0.00013.
Values sent between devices are 32-bit elements; how exact they have to be, the bound alone decides.
A program may use at most 64 MiB of HBM per device.

v0:
```python
import jax
import jax.numpy as jnp
import numpy as np
from jax import lax
from jax.sharding import PartitionSpec as P

SUBSTEPS = 8
CAP = 16
SN_DEV = 8


gamma_ratio = 1.4
courant = 0.02


def with_halo(x, sides, width):
    for axis, dim in sides:
        devices, length = (lax.axis_size(axis), x.shape[dim])
        up = [(i, (i + 1) % devices) for i in range(devices)]
        down = [(j, i) for i, j in up]
        last = lax.slice_in_dim(x, length - width, length, axis=dim)
        first = lax.slice_in_dim(x, 0, width, axis=dim)
        before = lax.ppermute(last, axis, up)
        after = lax.ppermute(first, axis, down)
        x = jnp.concatenate([before, x, after], axis=dim)
    return x


def gll_tables():
    gll_nodes = np.array([-1.0, -np.sqrt(0.2), np.sqrt(0.2), 1.0])
    weights = np.array([1.0, 5.0, 5.0, 1.0]) / 6.0
    bary_weights = np.array(
        [
            1.0
            / np.prod(
                [
                    gll_nodes[index_a] - gll_nodes[index_b]
                    for index_b in range(4)
                    if index_b != index_a
                ]
            )
            for index_a in range(4)
        ]
    )
    derivative = np.zeros((4, 4))
    for index_a in range(4):
        for index_b in range(4):
            if index_a != index_b:
                derivative[index_a, index_b] = (
                    bary_weights[index_b]
                    / bary_weights[index_a]
                    / (gll_nodes[index_a] - gll_nodes[index_b])
                )
        derivative[index_a, index_a] = -np.sum(derivative[index_a])
    return (jnp.asarray(derivative, jnp.float32), jnp.asarray(weights, jnp.float32))


def euler_flux(conserved, direction):
    density = conserved[0]
    normal_velocity = conserved[1 + direction] / density
    pressure = (gamma_ratio - 1.0) * (
        conserved[4]
        - 0.5
        * (conserved[1] * conserved[1] + conserved[2] * conserved[2] + conserved[3] * conserved[3])
        / density
    )
    flux_rows = [conserved[1 + direction]]
    for component in range(3):
        momentum_flux = conserved[1 + component] * normal_velocity
        if component == direction:
            momentum_flux = momentum_flux + pressure
        flux_rows.append(momentum_flux)
    flux_rows.append(normal_velocity * (conserved[4] + pressure))
    wave_speed = jnp.abs(normal_velocity) + jnp.sqrt(gamma_ratio * pressure / density)
    return (jnp.stack(flux_rows), wave_speed)


def rusanov(left_state, right_state, direction):
    left_flux, left_speed = euler_flux(left_state, direction)
    right_flux, right_speed = euler_flux(right_state, direction)
    fastest = jnp.maximum(left_speed, right_speed)
    return 0.5 * (left_flux + right_flux) - 0.5 * fastest * (right_state - left_state)


def mirrored(conserved):
    return jnp.concatenate([conserved[:3], -conserved[3:4], conserved[4:]], axis=0)


def node_index(node_axis, which):
    return (slice(None),) * node_axis + (which,)


def dg_rate(state, direction, flux_low, flux_high, derivative, weights):
    node_flux, wave_speed = euler_flux(state, direction)
    einsum_forms = ["ai,vijk...->vajk...", "aj,vijk...->viak...", "ak,vijk...->vija..."]
    volume = jnp.einsum(
        einsum_forms[direction], derivative, node_flux, precision=lax.Precision.HIGHEST
    )
    node_axis = 1 + direction
    low_index = node_index(node_axis, 0)
    high_index = node_index(node_axis, 3)
    volume = volume.at[low_index].add(-(flux_low - node_flux[low_index]) / weights[0])
    volume = volume.at[high_index].add((flux_high - node_flux[high_index]) / weights[3])
    return volume


def fv_rate(state, direction, flux_low, flux_high, weights):
    node_axis = 1 + direction
    lower_nodes = lax.slice_in_dim(state, 0, 3, axis=node_axis)
    upper_nodes = lax.slice_in_dim(state, 1, 4, axis=node_axis)
    inner_flux = rusanov(lower_nodes, upper_nodes, direction)
    interfaces = jnp.concatenate(
        [jnp.expand_dims(flux_low, node_axis), inner_flux, jnp.expand_dims(flux_high, node_axis)],
        axis=node_axis,
    )
    width_shape = [1] * state.ndim
    width_shape[node_axis] = 4
    widths = weights.reshape(width_shape)
    upper_faces = lax.slice_in_dim(interfaces, 1, 5, axis=node_axis)
    lower_faces = lax.slice_in_dim(interfaces, 0, 4, axis=node_axis)
    return (upper_faces - lower_faces) / widths


def dg_next(state, fluxes, derivative, weights):
    rate_sum = dg_rate(state, 0, fluxes[0], fluxes[1], derivative, weights)
    rate_sum = rate_sum + dg_rate(state, 1, fluxes[2], fluxes[3], derivative, weights)
    rate_sum = rate_sum + dg_rate(state, 2, fluxes[4], fluxes[5], derivative, weights)
    return state - courant * rate_sum


def fv_next(state, fluxes, weights):
    sub_state = state
    for substep in range(SUBSTEPS):
        rate_sum = fv_rate(sub_state, 0, fluxes[0], fluxes[1], weights)
        rate_sum = rate_sum + fv_rate(sub_state, 1, fluxes[2], fluxes[3], weights)
        rate_sum = rate_sum + fv_rate(sub_state, 2, fluxes[4], fluxes[5], weights)
        sub_state = sub_state - courant / SUBSTEPS * rate_sum
    return sub_state


def z_fluxes(state):
    z_low, z_high = (state[:, :, :, 0], state[:, :, :, 3])
    below_states = jnp.concatenate([mirrored(z_low[..., 0:1]), z_high[..., :-1]], axis=-1)
    z_flux_low = rusanov(below_states, z_low, 2)
    top_flux = rusanov(z_high[..., -1:], mirrored(z_high[..., -1:]), 2)
    z_flux_high = jnp.concatenate([z_flux_low[..., 1:], top_flux], axis=-1)
    return (z_flux_low, z_flux_high, top_flux)


def wall_face_loads(z_flux_low, top_flux, weights):
    face_weights = weights[:, None] * weights[None, :]
    bottom_load = -jnp.sum(
        face_weights[:, :, None, None] * z_flux_low[3, :, :, :, :, 0], axis=(0, 1)
    )
    top_load = jnp.sum(face_weights[:, :, None, None] * top_flux[3, :, :, :, :, 0], axis=(0, 1))
    return jnp.stack([bottom_load, top_load], axis=-1)


def limit_columns(state_cols, flux_cols, positions, capacity, weights):
    packed_state = (
        jnp.ones((320, capacity), jnp.float32).at[:, positions].set(state_cols, mode="drop")
    )
    packed_flux = (
        jnp.ones((480, capacity), jnp.float32).at[:, positions].set(flux_cols, mode="drop")
    )
    face_list = [
        packed_flux[80 * face : 80 * (face + 1)].reshape(5, 4, 4, capacity) for face in range(6)
    ]
    limited_state = fv_next(packed_state.reshape(5, 4, 4, 4, capacity), face_list, weights)
    return limited_state.reshape(320, capacity)


def on_device(state, limit_slot, wall_owner):
    derivative, weights = gll_tables()
    n_dev = lax.axis_size("dev")
    x_low, x_high = (state[:, 0], state[:, 3])
    x_rim = jnp.stack([x_low[:, :, :, 0], x_high[:, :, :, -1]], axis=3)
    x_around = with_halo(x_rim, (("group", 3),), 1)
    x_flux = rusanov(
        jnp.concatenate([x_around[:, :, :, 0:1], x_high], axis=3),
        jnp.concatenate([x_low, x_around[:, :, :, 3:4]], axis=3),
        0,
    )
    y_low, y_high = (state[:, :, 0], state[:, :, 3])
    y_rim = jnp.stack([y_low[:, :, :, :, 0], y_high[:, :, :, :, -1]], axis=4)
    y_around = with_halo(y_rim, (("dev", 4),), 1)
    y_flux = rusanov(
        jnp.concatenate([y_around[:, :, :, :, 0:1], y_high], axis=4),
        jnp.concatenate([y_low, y_around[:, :, :, :, 3:4]], axis=4),
        1,
    )
    z_flux_low, z_flux_high, top_flux = z_fluxes(state)
    fluxes = [
        x_flux[:, :, :, :-1],
        x_flux[:, :, :, 1:],
        y_flux[:, :, :, :, :-1],
        y_flux[:, :, :, :, 1:],
        z_flux_low,
        z_flux_high,
    ]
    face_load = wall_face_loads(z_flux_low, top_flux, weights)
    load_flat = face_load.reshape(-1)
    owner_flat = wall_owner.reshape(-1)
    all_nodes = SN_DEV * lax.axis_size("group") * n_dev
    matches = owner_flat[:, None] == jnp.arange(all_nodes, dtype=jnp.int32)[None, :]
    partial_value = jnp.sum(jnp.where(matches, load_flat[:, None], 0.0), axis=0)
    wall_loads = lax.psum_scatter(partial_value, ("group", "dev"), scatter_dimension=0, tiled=True)
    dg_state = dg_next(state, fluxes, derivative, weights)
    elements = limit_slot.size
    state_cols = state.reshape(320, elements)
    flux_cols = jnp.stack([face.reshape(80, elements) for face in fluxes]).reshape(480, elements)
    slot_flat = limit_slot.reshape(elements)
    troubled = slot_flat >= 0
    capacity = n_dev * CAP
    order_rank = jnp.cumsum(troubled.astype(jnp.int32)) - 1
    positions = jnp.where(troubled, order_rank, capacity)
    results = limit_columns(state_cols, flux_cols, positions, capacity, weights)
    limited = jnp.take(results, jnp.clip(positions, 0, capacity - 1), axis=1)
    state_next = jnp.where(troubled[None, :], limited, dg_state.reshape(320, elements)).reshape(
        state.shape
    )
    return (state_next, wall_loads)


def solution(mesh):
    in_specs = (
        P(None, None, None, None, "group", "dev", None),
        P("group", "dev", None),
        P("group", "dev", None),
    )
    out_specs = (P(None, None, None, None, "group", "dev", None), P(("group", "dev")))
    return jax.shard_map(
        on_device, mesh=mesh, in_specs=in_specs, out_specs=out_specs, check_vma=False
    )
```

profile of v0, /device:TPU:0, one launch (start us, length us, event | category | flops | bytes accessed | tf_op | source)
XLA Modules:
  0.0 274.4 jit_solution(12072246452089902455)
XLA Ops:
  0.6 1.3 copy.733
  3.7 1.9 collective-permute-start.1
  6.4 2.3 collective-permute-start.2
  9.5 3.0 %collective-permute-start.3 = (f32[5,4,4,2,1,128]{5,2,4,3,0,1:T(4,128)}, f32[5,4,4,2,1,128]{5,2,4,3,0,1:T(4,128)S(1)}, u32[]{:S(2)}, u32[]{:S(2)}) collective-permute-start(f32[5,4,4,2,1,128]{5,2,4,3,0,1:T(4,128)} %slice.2686), channel_id=1, source_target_pairs={{1,0},{2,1},{3,2},{4,3},{5,4},{6,5},{7,6},{0,7},{9,8},{10,9},{11,1... | collective-permute-start | bytes 245768 | tf_op jit(solution)/shard_map/ppermute | solution.py:24
  14.9 2.9 %scatter_custom_fusion = f32[320,128]{0,1:T(8,128)S(1)} fusion(s32[512]{0:T(512)S(1)} %bitcast.670, f32[320,512]{0,1:T(8,128)S(1)} %copy.731, f32[]{:T(128)} %constant.276.clone.1), kind=kCustom, calls=%fused_computation.3 | custom fusion | bytes 950276 | tf_op jit(solution)/shard_map/scatter | solution.py:161
  17.9 0.8 multiply_bitcast_fusion.9
  21.0 0.8 fusion.224
  23.0 0.8 concatenate.252
  24.6 0.8 slice.2714
  27.0 1.6 fusion.10
  30.4 0.8 pad_maximum_fusion.52
  32.2 1.2 fusion.2
  33.4 0.8 slice.3006
  34.2 0.9 copy.1059
  39.5 1.9 fusion.84
  42.5 0.9 constant_dynamic-update-slice_fusion.47
  43.4 0.8 constant_dynamic-update-slice_fusion.43
  44.2 0.8 constant_dynamic-update-slice_fusion.42
  45.3 0.8 constant_dynamic-update-slice_fusion.46
  46.1 0.8 constant_dynamic-update-slice_fusion.45
  47.6 1.3 fusion.79
  48.9 1.1 copy.871
  56.6 0.8 mul.3742
  57.4 0.8 mul.3748.clone
  58.2 0.8 mul.3749
  59.3 0.8 stack_reshape.20
  61.3 2.4 fusion.8
  64.8 1.9 copy.872
  69.4 1.4 copy.868
  70.8 1.2 copy.869
  77.3 38.0 %all-reduce = f32[256]{0:T(256)} all-reduce(f32[256]{0:T(256)S(1)} %select_reduce_fusion), channel_id=2, replica_groups=mesh['group'=4,'dev'=8] {'group','dev'}, use_global_device_ids=true, to_apply=%region_7.8.clone | all-reduce | flops 256 | bytes 2048
  119.0 1.2 fusion.81
  120.2 2.0 multiply_add_fusion
  122.3 7.4 %scatter-add.26 = f32[5,4,4,4,2,2,128]{6,3,5,4,2,0,1:T(4,128)} dynamic-update-slice(f32[5,4,4,4,2,2,128]{6,3,5,4,2,0,1:T(4,128)} %bitcast.631, f32[5,4,4,1,2,2,128]{6,3,5,4,2,0,1:T(1,128)} %multiply_add_fusion, s32[]{:T(128)} %constant.272.clone.1, s32[]{:T(128)} %constant.272.clone.1, s32[]{:T(128)} %constant.272.clone.1, s32[]{:T(128)} %constant.272.clone.1, s32[]{:T(128)} %constant.272.clone.1, ...) | dynamic-update-slice | bytes 327684 | tf_op jit(solution)/shard_map/scatter-add | solution.py:102
  129.7 2.6 fusion.43
  132.3 7.4 %scatter-add.29 = f32[5,4,4,4,2,2,128]{6,3,5,4,2,0,1:T(4,128)} dynamic-update-slice(f32[5,4,4,4,2,2,128]{6,3,5,4,2,0,1:T(4,128)} %scatter-add.26, f32[5,4,4,1,2,2,128]{6,3,5,4,2,0,1:T(1,128)} %fusion.43, s32[]{:T(128)} %constant.272.clone.1, s32[]{:T(128)} %constant.272.clone.1, s32[]{:T(128)} %constant.272.clone.1, s32[]{:T(128)} %constant.282.clone.1, s32[]{:T(128)} %constant.272.clone.1, ...) | dynamic-update-slice | bytes 327684 | tf_op jit(solution)/shard_map/scatter-add | solution.py:103
  140.4 1.7 fusion.77
  152.9 2.5 copy.776
  155.4 3.2 %scatter_custom_fusion.1 = f32[480,128]{0,1:T(8,128)S(1)} fusion(s32[512]{0:T(512)} %bitcast.671, f32[512,480]{1,0:T(8,128)} %copy.776, f32[]{:T(128)} %constant.276.clone.1), kind=kCustom, calls=%fused_computation.566 | custom fusion | bytes 246272 | tf_op jit(solution)/shard_map/scatter | solution.py:164
  173.6 1.1 fusion.75
  174.7 1.0 fusion.129
  175.7 1.0 fusion.131
  190.4 1.1 fusion.73
  191.4 1.0 fusion.125
  192.5 1.0 fusion.127
  207.1 1.1 fusion.71
  208.2 1.0 fusion.121
  209.2 1.0 fusion.123
  223.8 1.1 fusion.69
  224.9 1.0 fusion.117
  225.9 1.0 fusion.119
  240.5 1.1 fusion.67
  241.6 1.0 fusion.113
  242.7 1.0 fusion.115
  257.3 1.1 fusion.65
  258.4 1.0 fusion.109
  259.4 1.0 fusion.111
  262.6 2.5 gather_fusion
  265.2 2.2 copy.833
  267.4 1.5 gather.7
  268.9 1.2 fusion.55
  270.1 1.1 fusion.49
  271.5 0.8 copy-done.1
  273.0 1.2 copy.877
  (503 shorter events, 138.3 us)
Async XLA Ops:
  2.0 3.7 %copy-start = (f32[5,4,4,4,2,2,128]{6,5,4,3,2,1,0:T(2,128)S(1)}, f32[5,4,4,4,2,2,128]{6,5,4,3,2,1,0:T(2,128)}, u32[]{:S(2)}) copy-start(f32[5,4,4,4,2,2,128]{6,5,4,3,2,1,0:T(2,128)} %param.17) | copy-start | bytes 1966084
  2.6 141.9 %collective-permute-start = (f32[5,4,4,1,2,128]{5,2,4,3,1,0:T(4,128)}, f32[5,4,4,1,2,128]{5,2,4,3,1,0:T(4,128)S(1)}, u32[]{:S(2)}, u32[]{:S(2)}) collective-permute-start(f32[5,4,4,1,2,128]{5,2,4,3,1,0:T(4,128)} %slice.2650), channel_id=1, source_target_pairs={{0,8},{8,16},{16,24},{24,0},{1,9},{9,17},{17,25},{25,1},{2,10},{10... | collective-permute-start | bytes 245768 | tf_op jit(solution)/shard_map/ppermute | solution.py:23
  3.7 140.8 %collective-permute-start.1 = (f32[5,4,4,1,2,128]{5,2,4,3,1,0:T(4,128)}, f32[5,4,4,1,2,128]{5,2,4,3,1,0:T(4,128)S(1)}, u32[]{:S(2)}, u32[]{:S(2)}) collective-permute-start(f32[5,4,4,1,2,128]{5,2,4,3,1,0:T(4,128)} %slice.2662), channel_id=1, source_target_pairs={{8,0},{16,8},{24,16},{0,24},{9,1},{17,9},{25,17},{1,25},{10,2},{18... | collective-permute-start | bytes 245768 | tf_op jit(solution)/shard_map/ppermute | solution.py:24
  6.4 141.2 %collective-permute-start.2 = (f32[5,4,4,2,1,128]{5,2,4,3,0,1:T(4,128)}, f32[5,4,4,2,1,128]{5,2,4,3,0,1:T(4,128)S(1)}, u32[]{:S(2)}, u32[]{:S(2)}) collective-permute-start(f32[5,4,4,2,1,128]{5,2,4,3,0,1:T(4,128)} %slice.2675), channel_id=1, source_target_pairs={{0,1},{1,2},{2,3},{3,4},{4,5},{5,6},{6,7},{7,0},{8,9},{9,10},{10,1... | collective-permute-start | bytes 245768 | tf_op jit(solution)/shard_map/ppermute | solution.py:23
  9.4 3.6 %copy-start.83 = (s32[2,2,128]{2,1,0:T(2,128)S(1)}, s32[2,2,128]{2,1,0:T(2,128)}, u32[]{:S(2)}) copy-start(s32[2,2,128]{2,1,0:T(2,128)} %param.18) | copy-start | bytes 6148
  9.5 138.2 %collective-permute-start.3 = (f32[5,4,4,2,1,128]{5,2,4,3,0,1:T(4,128)}, f32[5,4,4,2,1,128]{5,2,4,3,0,1:T(4,128)S(1)}, u32[]{:S(2)}, u32[]{:S(2)}) collective-permute-start(f32[5,4,4,2,1,128]{5,2,4,3,0,1:T(4,128)} %slice.2686), channel_id=1, source_target_pairs={{1,0},{2,1},{3,2},{4,3},{5,4},{6,5},{7,6},{0,7},{9,8},{10,9},{11,1... | collective-permute-start | bytes 245768 | tf_op jit(solution)/shard_map/ppermute | solution.py:24
  13.0 1.0 copy-start.77
  14.9 2.9 %copy-start.84 = (s32[512,1]{0,1:T(1,128)}, s32[512,1]{0,1:T(1,128)S(1)}, u32[]{:S(2)}) copy-start(s32[512,1]{0,1:T(1,128)S(1)} %get-tuple-element.477) | copy-start | bytes 6148
  20.3 1.5 copy-start.10
  20.3 9.8 %copy-start.38 = (f32[1,4,4,2,2,1]{5,4,3,2,1,0:T(2,128)}, f32[1,4,4,2,2,1]{5,4,3,2,1,0:T(2,128)S(1)}, u32[]{:S(2)}) copy-start(f32[1,4,4,2,2,1]{5,4,3,2,1,0:T(2,128)S(1)} %fusion.157) | copy-start | bytes 772
  20.3 9.8 %copy-start.40 = (f32[1,4,4,2,2,1]{5,4,3,2,1,0:T(2,128)}, f32[1,4,4,2,2,1]{5,4,3,2,1,0:T(2,128)S(1)}, u32[]{:S(2)}) copy-start(f32[1,4,4,2,2,1]{5,4,3,2,1,0:T(2,128)S(1)} %slice_bitcast_fusion.7) | copy-start | bytes 772
  27.0 1.6 copy-start.6
  28.7 0.8 copy-start.3
  29.5 0.9 copy-start.11
  32.1 1.3 copy-start.8
  32.2 1.3 copy-start.9
  36.4 1.3 copy-start.50
  37.7 0.8 copy-start.20
  37.9 0.9 copy-start.17
  38.6 0.9 copy-start.12
  38.6 0.9 copy-start.39
  38.6 0.9 copy-start.41
  38.7 2.7 copy-start.36
  41.4 0.9 copy-start.48
  41.6 17.4 %copy-start.18 = (f32[5,4,4,2,2,127]{5,4,3,2,0,1:T(2,128)}, f32[5,4,4,2,2,127]{5,4,3,2,0,1:T(2,128)S(1)}, u32[]{:S(2)}) copy-start(f32[5,4,4,2,2,127]{5,4,3,2,0,1:T(2,128)S(1)} %slice.2708) | copy-start | bytes 487684
  46.1 1.5 copy-start.44
  48.9 10.2 %copy-start.13 = (f32[5,4,4,2,2,1]{5,4,3,2,0,1:T(2,128)}, f32[5,4,4,2,2,1]{5,4,3,2,0,1:T(2,128)S(1)}, u32[]{:S(2)}) copy-start(f32[5,4,4,2,2,1]{5,4,3,2,0,1:T(2,128)S(1)} %fusion.79) | copy-start | bytes 3844
  48.9 1.1 copy-start.61
  52.9 0.9 copy-start.58
  53.7 0.8 copy-start.64
  55.2 1.4 copy-start.22
  59.3 0.9 copy-start.79
  59.3 1.9 copy-start.76
  64.0 0.8 copy-start.2
  72.7 1.3 copy-start.27
  117.4 1.4 copy-start.47
  117.4 1.4 copy-start.23
  117.4 1.4 copy-start.25
  118.1 0.8 copy-start.37
  119.0 1.2 copy-start.24
  122.3 7.4 %copy-start.19 = (f32[5,4,4,2,2,127]{5,4,3,2,0,1:T(2,128)S(1)}, f32[5,4,4,2,2,127]{5,4,3,2,0,1:T(2,128)}, u32[]{:S(2)}) copy-start(f32[5,4,4,2,2,127]{5,4,3,2,0,1:T(2,128)} %copy-done.18) | copy-start | bytes 487684
  129.6 10.0 %copy-start.74 = (s32[4,128]{1,0:T(4,128)S(1)}, s32[4,128]{1,0:T(4,128)}, u32[]{:S(2)}) copy-start(s32[4,128]{1,0:T(4,128)} %copy-done.73) | copy-start | bytes 6148
  129.6 10.0 %copy-start.78 = (pred[2,2,128]{2,1,0:T(4,128)(4,1)S(1)}, pred[2,2,128]{2,1,0:T(4,128)(4,1)}, u32[]{:S(2)}) copy-start(pred[2,2,128]{2,1,0:T(4,128)(4,1)} %copy-done.77) | copy-start | bytes 1540
  132.3 7.4 %copy-start.85 = (s32[2,2]{1,0:T(2,128)S(1)}, s32[2,2]{1,0:T(2,128)}, u32[]{:S(2)}) copy-start(s32[2,2]{1,0:T(2,128)} %reshape.1231) | copy-start | bytes 52
  132.3 7.5 %copy-start.86 = (f32[256]{0:T(256)S(1)}, f32[256]{0:T(256)}, u32[]{:S(2)}) copy-start(f32[256]{0:T(256)} %all-reduce) | copy-start | bytes 3076
  132.3 8.1 %copy-start.51 = (f32[5,4,4,3,128]{4,3,2,1,0:T(4,128)S(1)}, f32[5,4,4,3,128]{4,3,2,1,0:T(4,128)}, u32[]{:S(2)}) copy-start(f32[5,4,4,3,128]{4,3,2,1,0:T(4,128)} %get-tuple-element.447) | copy-start | bytes 368644
  140.4 1.7 copy-start.63
  140.4 1.7 copy-start.65
  140.4 1.7 copy-start.71
  142.1 0.9 copy-start.60
  142.2 1.0 copy-start.67
  142.2 0.9 copy-start.72
  149.5 1.4 copy-start.31
  150.2 1.0 copy-start.29
  150.2 1.1 copy-start.30
  151.2 0.9 copy-start.26
  158.9 0.9 copy-start.43
  159.0 0.9 copy-start.28
  159.1 0.9 copy-start.42
  268.9 2.4 copy-start.7
  268.9 2.5 copy-start.5
  270.1 1.2 slice-start
  270.1 1.2 copy-start.15
  271.2 1.1 copy-start.1
  (29 other events, 20.7 us)
where the time goes:
time: 280 us; the launch traced here: 274 us
  other arithmetic  142 us (51%)
  local copies, waits for them, and re-layouts  79.4 us (28%)
  blocking collectives  38 us (14%)
  starting transfers between devices  7.75 us (3%)
  matrix products  5.28 us (2%)
    unnamed x142, other arithmetic  63.2 us
    unnamed x1, blocking collectives  38 us
    sub x29, other arithmetic, rusanov(): 0.5 * (left_flux + right_flux) - 0.5 * fastest * (right_state - left_state)  26.9 us
    unnamed x196, local copies, waits for them, and re-layouts  26 us
    another operation x49, other arithmetic, euler_flux(): return (jnp.stack(flux_rows), wave_speed)  23.3 us
    mul x26, other arithmetic, rusanov(): 0.5 * fastest * (right_state - left_state)  14.6 us
    scatter-add x1, local copies, waits for them, and re-layouts, dg_rate(): volume.at[high_index].add((flux_high - node_flux[high_index]) / weights[3])  7.39 us
    scatter-add x1, local copies, waits for them, and re-layouts, dg_rate(): volume.at[low_index].add(-(flux_low - node_flux[low_index]) / weights[0])  7.38 us
  transfers between devices with their start and end apart: 4, of which 0 were waited for; matrix products, arithmetic and copies ran while one was open for 30% of the time, Pallas kernels for 0%

commit v1 on v0

v1 whole, which is shorter than its diff:
```python
import functools

import jax
import jax.numpy as jnp
import numpy as np
from jax import lax
from jax.experimental import pallas as pl
from jax.experimental.pallas import tpu as pltpu
from jax.sharding import PartitionSpec as P

SUBSTEPS = 8
CAP = 16
SN_DEV = 8
LANES = 128
MESH = pl.DeviceIdType.MESH

gamma_ratio = 1.4
courant = 0.02


def gll_tables():
    nodes = np.array([-1.0, -np.sqrt(0.2), np.sqrt(0.2), 1.0])
    weights = np.array([1.0, 5.0, 5.0, 1.0]) / 6.0
    bary = np.array(
        [1.0 / np.prod([nodes[a] - nodes[b] for b in range(4) if b != a]) for a in range(4)]
    )
    derivative = np.zeros((4, 4))
    for a in range(4):
        for b in range(4):
            if a != b:
                derivative[a, b] = bary[b] / bary[a] / (nodes[a] - nodes[b])
        derivative[a, a] = -np.sum(derivative[a])
    return derivative, weights


DERIV, WEIGHTS = gll_tables()
VOLUME = DERIV.copy()
VOLUME[0, 0] += 1.0 / WEIGHTS[0]
VOLUME[3, 3] -= 1.0 / WEIGHTS[3]


def primitives(u):
    inv = 1.0 / u[0]
    p = (gamma_ratio - 1.0) * (u[4] - 0.5 * (u[1] * u[1] + u[2] * u[2] + u[3] * u[3]) * inv)
    return inv, p


def sound(inv, p):
    return jnp.sqrt(gamma_ratio * p * inv)


def flux_of(u, inv, p, d):
    v = u[1 + d] * inv
    rows = [u[1 + d]]
    for c in range(3):
        m = u[1 + c] * v
        rows.append(m + p if c == d else m)
    rows.append(v * (u[4] + p))
    return rows, v


def flux_speed(u, d):
    inv, p = primitives(u)
    rows, v = flux_of(u, inv, p, d)
    return rows, jnp.abs(v) + sound(inv, p)


def combine(ul, fl, sl, ur, fr, sr):
    half = 0.5 * jnp.maximum(sl, sr)
    return [0.5 * (fl[c] + fr[c]) - half * (ur[c] - ul[c]) for c in range(5)]


def rusanov(ul, ur, d):
    fl, sl = flux_speed(ul, d)
    fr, sr = flux_speed(ur, d)
    return combine(ul, fl, sl, ur, fr, sr)


def kernel(
    n_group,
    n_dev,
    capacity,
    state_ref,
    slot_ref,
    owner_ref,
    out_ref,
    load_ref,
    fx_ref,
    fy_ref,
    fz_ref,
    send_halo,
    recv_halo,
    part1,
    got1,
    part2,
    got2,
    hs,
    hr,
    s1,
    r1,
    s2,
    r2,
):
    gi = lax.axis_index("group")
    di = lax.axis_index("dev")

    barrier = pltpu.get_barrier_semaphore()
    for off in range(1, n_dev):
        pl.semaphore_signal(
            barrier, inc=1, device_id=(gi, lax.rem(di + off, n_dev)), device_id_type=MESH
        )
    for off in range(1, n_group):
        pl.semaphore_signal(
            barrier, inc=1, device_id=(lax.rem(gi + off, n_group), di), device_id_type=MESH
        )

    sub = lax.broadcasted_iota(jnp.int32, (8, LANES), 0)
    lane = lax.broadcasted_iota(jnp.int32, (8, LANES), 1)
    lower = sub < 4
    first = (lax.rem(sub, 4) < 2, lax.rem(sub, 2) < 1)
    shift = (2, 1)

    def tile(ref, index):
        return ref[pl.ds(pl.multiple_of(index * 8, 8), 8), :]

    def put(ref, index, value):
        ref[pl.ds(pl.multiple_of(index * 8, 8), 8), :] = value

    def node(c, i, j, kp):
        return ((c * 4 + i) * 4 + j) * 2 + kp

    def face(c, d, side, t, kp):
        return node(c, 3 * side, t, kp) if d == 0 else node(c, t, 3 * side, kp)

    roll = lambda x, n: pltpu.roll(x, n % 8, 0)

    def pack(t, carry):
        for d in range(2):
            for c in range(5):
                hi = [tile(state_ref, face(c, d, 1, t, kp)) for kp in range(2)]
                lo = [tile(state_ref, face(c, d, 0, t, kp)) for kp in range(2)]
                put(send_halo.at[2 * d + 1], c * 4 + t, jnp.where(first[d], roll(hi[0], -shift[d]), hi[1]))
                put(send_halo.at[2 * d], c * 4 + t, jnp.where(first[d], lo[0], roll(lo[1], shift[d])))
        return carry

    lax.fori_loop(0, 4, pack, 0)

    pl.semaphore_wait(barrier, n_dev - 1 + n_group - 1)

    halo_copies = []
    for d in range(2):
        for side in range(2):
            step = 1 if side == 1 else -1
            if d == 0:
                target = (lax.rem(gi + step + n_group, n_group), di)
            else:
                target = (gi, lax.rem(di + step + n_dev, n_dev))
            slot = 2 * d + side
            arrive = 2 * d + 1 - side
            copy = pltpu.make_async_remote_copy(
                src_ref=send_halo.at[slot],
                dst_ref=recv_halo.at[arrive],
                send_sem=hs.at[slot],
                recv_sem=hr.at[arrive],
                device_id=target,
                device_id_type=MESH,
            )
            copy.start()
            halo_copies.append(copy)

    wij = [[float(WEIGHTS[i] * WEIGHTS[j]) for j in range(4)] for i in range(4)]
    weight_node = lambda a: jnp.where((a == 0) | (a == 3), float(WEIGHTS[0]), float(WEIGHTS[1]))

    def z_faces(q, load):
        i, j = q // 4, q % 4
        u0 = [tile(state_ref, node(c, i, j, 0)) for c in range(5)]
        u3 = [tile(state_ref, node(c, i, j, 1)) for c in range(5)]
        below = []
        for c in range(5):
            mirror = -u0[c] if c == 3 else u0[c]
            below.append(jnp.where(lane == 0, mirror, pltpu.roll(roll(u3[c], 4), 1, 1)))
        low = rusanov(below, u0, 2)
        inv, p = primitives(u3)
        v = u3[3] * inv
        top = u3[3] * v + p + (jnp.abs(v) + sound(inv, p)) * u3[3]
        for c in range(5):
            high = pltpu.roll(roll(low[c], 4), LANES - 1, 1)
            high = jnp.where(lane == LANES - 1, top if c == 3 else 0.0, high)
            both = jnp.where(lower, low[c], high)
            put(fz_ref, node(c, i, j, 0), both)
            put(fz_ref, node(c, i, j, 1), both)
            if c == 3:
                load = load + (weight_node(i) * weight_node(j)) * both
        return load

    load = lax.fori_loop(0, 16, z_faces, jnp.zeros((8, LANES), jnp.float32))

    value = jnp.where(lower, -load, load)
    wall_lane = jnp.where(lower, 0, LANES - 1)
    value = jnp.sum(jnp.where(lane == wall_lane, value, 0.0), axis=1, keepdims=True)
    owner = jnp.zeros((8, LANES), jnp.int32)
    for s in range(2):
        for x in range(2):
            for y in range(2):
                owner = jnp.where(sub == s * 4 + x * 2 + y, owner_ref[x, y, s], owner)
    group_base = (lane // SN_DEV) * (n_dev * SN_DEV) + lax.rem(lane, SN_DEV)
    used = lane < n_group * SN_DEV
    copies1 = []
    for off in range(n_dev):
        peer = lax.rem(di + off, n_dev)
        match = (owner == group_base + peer * SN_DEV) & used
        part1[off] = jnp.where(match, value, 0.0)
        if off:
            copy = pltpu.make_async_remote_copy(
                src_ref=part1.at[off],
                dst_ref=got1.at[off],
                send_sem=s1.at[off],
                recv_sem=r1.at[off],
                device_id=(gi, peer),
                device_id_type=MESH,
            )
            copy.start()
            copies1.append(copy)

    dt = courant
    vol = [[float(VOLUME[a, b]) for b in range(4)] for a in range(4)]

    def node_flux(i, j, kp, d):
        u = [tile(state_ref, node(c, i, j, kp)) for c in range(5)]
        inv, p = primitives(u)
        return u, flux_of(u, inv, p, d)[0]

    def x_part(q, carry):
        j, kp = q // 2, q % 2
        cols = [node_flux(i, j, kp, 0) for i in range(4)]
        for c in range(5):
            for a in range(4):
                rate = sum(vol[a][b] * cols[b][1][c] for b in range(4))
                put(out_ref, node(c, a, j, kp), cols[a][0][c] - dt * rate)
        return carry

    lax.fori_loop(0, 8, x_part, 0)

    def y_part(q, carry):
        i, kp = q // 2, q % 2
        cols = [node_flux(i, j, kp, 1) for j in range(4)]
        for c in range(5):
            for a in range(4):
                rate = sum(vol[a][b] * cols[b][1][c] for b in range(4))
                index = node(c, i, a, kp)
                put(out_ref, index, tile(out_ref, index) - dt * rate)
        return carry

    lax.fori_loop(0, 8, y_part, 0)

    def halves(a, b):
        return jnp.where(lower, -dt * vol[a[0]][a[1]], -dt * vol[b[0]][b[1]])

    zc = [
        [halves((0, 0), (1, 1)), halves((0, 1), (1, 0)), halves((0, 2), (1, 3)), halves((0, 3), (1, 2))],
        [halves((2, 0), (3, 1)), halves((2, 1), (3, 0)), halves((2, 2), (3, 3)), halves((2, 3), (3, 2))],
    ]
    zf = [
        jnp.where(lower, dt / float(WEIGHTS[0]), 0.0),
        jnp.where(lower, 0.0, -dt / float(WEIGHTS[3])),
    ]

    def z_part(q, carry):
        i, j = q // 4, q % 4
        f = [node_flux(i, j, kp, 2)[1] for kp in range(2)]
        for c in range(5):
            t0, t1 = f[0][c], f[1][c]
            q0, q1 = roll(t0, 4), roll(t1, 4)
            surface = tile(fz_ref, node(c, i, j, 0))
            for kp in range(2):
                k = zc[kp]
                rate = k[0] * t0 + k[1] * q0 + k[2] * t1 + k[3] * q1 + zf[kp] * surface
                index = node(c, i, j, kp)
                put(out_ref, index, tile(out_ref, index) + rate)
        return carry

    lax.fori_loop(0, 16, z_part, 0)

    for copy in copies1:
        copy.wait()
    total = part1[0]
    for off in range(1, n_dev):
        total = total + got1[off]
    part2[...] = total
    copies2 = []
    for off in range(1, n_group):
        copy = pltpu.make_async_remote_copy(
            src_ref=part2,
            dst_ref=got2.at[off],
            send_sem=s2.at[off],
            recv_sem=r2.at[off],
            device_id=(lax.rem(gi + off, n_group), di),
            device_id_type=MESH,
        )
        copy.start()
        copies2.append(copy)

    for copy in halo_copies:
        copy.wait()

    face_scale = dt / float(WEIGHTS[0])

    def xy_faces(t, carry):
        for d in range(2):
            m, sh = first[d], shift[d]
            fref = (fx_ref, fy_ref)[d]
            own_lo = [tile(send_halo.at[2 * d], c * 4 + t) for c in range(5)]
            own_hi = [tile(send_halo.at[2 * d + 1], c * 4 + t) for c in range(5)]
            got_lo = [tile(recv_halo.at[2 * d], c * 4 + t) for c in range(5)]
            got_hi = [tile(recv_halo.at[2 * d + 1], c * 4 + t) for c in range(5)]
            left, right = [], []
            for c in range(5):
                hi = [tile(state_ref, face(c, d, 1, t, kp)) for kp in range(2)]
                lo = [tile(state_ref, face(c, d, 0, t, kp)) for kp in range(2)]
                left.append(jnp.where(m, hi[0], roll(hi[1], sh)))
                right.append(jnp.where(m, roll(lo[0], -sh), lo[1]))
            flo = rusanov(got_lo, own_lo, d)
            fin = rusanov(left, right, d)
            fhi = rusanov(own_hi, got_hi, d)
            for c in range(5):
                down, up = roll(fin[c], -sh), roll(fin[c], sh)
                values = [
                    [jnp.where(m, flo[c], up), jnp.where(m, roll(flo[c], -sh), fin[c])],
                    [jnp.where(m, fin[c], roll(fhi[c], sh)), jnp.where(m, down, fhi[c])],
                ]
                for side in range(2):
                    for kp in range(2):
                        val = values[side][kp]
                        if d == 0:
                            put(fref, ((c * 2 + side) * 4 + t) * 2 + kp, val)
                        else:
                            put(fref, ((c * 4 + t) * 2 + side) * 2 + kp, val)
                        index = face(c, d, side, t, kp)
                        scaled = face_scale * val
                        old = tile(out_ref, index)
                        put(out_ref, index, old - scaled if side else old + scaled)
        return carry

    lax.fori_loop(0, 4, xy_faces, 0)

    def split(x):
        hi = x.astype(jnp.bfloat16)
        return hi, (x - hi.astype(jnp.float32)).astype(jnp.bfloat16)

    kmod = lax.rem(sub, 4)
    k_first, k_last = kmod == 0, kmod == 3
    edge, inner = 1.0 / float(WEIGHTS[0]), 1.0 / float(WEIGHTS[1])
    sub_dt = courant / SUBSTEPS
    wk = jnp.where(k_first | k_last, sub_dt * edge, sub_dt * inner)
    wj = [
        jnp.where(lower, sub_dt * edge, sub_dt * inner),
        jnp.where(lower, sub_dt * inner, sub_dt * edge),
    ]
    wi = [sub_dt * edge, sub_dt * inner, sub_dt * inner, sub_dt * edge]

    for block in range(-(-capacity // LANES)):
        base = block * LANES
        rank = lax.broadcasted_iota(jnp.int32, (LANES, LANES), 0) + base
        slots = [slot_ref[e // 2, pl.ds(e % 2, 1), :] for e in range(4)]
        onehot = jnp.concatenate(
            [jnp.where(rank == s, 1.0, 0.0).astype(jnp.bfloat16) for s in slots], axis=1
        )

        def gather(ref, rows):
            x = jnp.concatenate(
                [ref[pl.ds(e, rows, stride=4), :] for e in range(4)], axis=1
            )
            dims = (((1,), (1,)), ((), ()))
            hi, mid = split(x)
            return lax.dot_general(
                hi, onehot, dims, preferred_element_type=jnp.float32
            ) + lax.dot_general(mid, onehot, dims, preferred_element_type=jnp.float32)

        packed = gather(state_ref, 320)
        occupied = packed[0:1, :] > 0.25
        px = gather(fx_ref, 160)
        py = gather(fy_ref, 160)
        pz = gather(fz_ref, 320)
        cut = lambda a, t: a[8 * t : 8 * t + 8]
        blank = (1.0, 0.0, 0.0, 0.0, 2.5)
        start = tuple(
            jnp.where(occupied, cut(packed, c * 8 + t), blank[c])
            for c in range(5)
            for t in range(8)
        )

        def substep(_, flat):
            u = [[flat[c * 8 + t] for c in range(5)] for t in range(8)]
            prim = [primitives(u[t]) for t in range(8)]
            cs = [sound(*prim[t]) for t in range(8)]
            new = [list(u[t]) for t in range(8)]

            def fluxes(d):
                out = []
                for t in range(8):
                    rows, v = flux_of(u[t], prim[t][0], prim[t][1], d)
                    out.append((rows, jnp.abs(v) + cs[t]))
                return out

            f = fluxes(0)
            for jp in range(2):
                g = [[cut(px, (c * 2 + 0) * 2 + jp) for c in range(5)]]
                for a in range(3):
                    l, r = a * 2 + jp, (a + 1) * 2 + jp
                    g.append(combine(u[l], f[l][0], f[l][1], u[r], f[r][0], f[r][1]))
                g.append([cut(px, (c * 2 + 1) * 2 + jp) for c in range(5)])
                for a in range(4):
                    t = a * 2 + jp
                    for c in range(5):
                        new[t][c] = new[t][c] - wi[a] * (g[a + 1][c] - g[a][c])

            f = fluxes(1)
            for i in range(4):
                t0, t1 = 2 * i, 2 * i + 1
                rolled = []
                for t in (t0, t1):
                    rolled.append(
                        (
                            [roll(x, 4) for x in u[t]],
                            [roll(x, 4) for x in f[t][0]],
                            roll(f[t][1], 4),
                        )
                    )
                ra, rb = rolled
                mix = lambda a, b: [jnp.where(lower, x, y) for x, y in zip(a, b)]
                ga = combine(
                    u[t0], f[t0][0], f[t0][1],
                    mix(ra[0], rb[0]), mix(ra[1], rb[1]), jnp.where(lower, ra[2], rb[2]),
                )
                gb = combine(u[t1], f[t1][0], f[t1][1], rb[0], rb[1], rb[2])
                for c in range(5):
                    bound = cut(py, c * 4 + i)
                    high1 = jnp.where(lower, gb[c], bound)
                    back0, back1 = roll(ga[c], 4), roll(high1, 4)
                    low0 = jnp.where(lower, bound, back0)
                    low1 = jnp.where(lower, back0, back1)
                    new[t0][c] = new[t0][c] - wj[0] * (ga[c] - low0)
                    new[t1][c] = new[t1][c] - wj[1] * (high1 - low1)

            f = fluxes(2)
            for t in range(8):
                g = combine(
                    u[t], f[t][0], f[t][1],
                    [roll(x, -1) for x in u[t]], [roll(x, -1) for x in f[t][0]], roll(f[t][1], -1),
                )
                for c in range(5):
                    bound = cut(pz, c * 8 + t)
                    high = jnp.where(k_last, bound, g[c])
                    low = jnp.where(k_first, bound, roll(high, 1))
                    new[t][c] = new[t][c] - wk * (high - low)
            return tuple(new[t][c] for c in range(5) for t in range(8))

        final = lax.fori_loop(0, SUBSTEPS, substep, start)
        result = jnp.concatenate([jnp.where(occupied, x, 0.0) for x in final], axis=0)
        hi, mid = split(result)
        dims = (((1,), (0,)), ((), ()))
        spread = lax.dot_general(
            hi, onehot, dims, preferred_element_type=jnp.float32
        ) + lax.dot_general(mid, onehot, dims, preferred_element_type=jnp.float32)
        for e in range(4):
            rows = pl.ds(e, 320, stride=4)
            here = (slots[e] >= base) & (slots[e] < base + LANES)
            out_ref[rows, :] = jnp.where(
                here, spread[:, e * LANES : (e + 1) * LANES], out_ref[rows, :]
            )

    for copy in copies2:
        copy.wait()
    total = part2[...]
    for off in range(1, n_group):
        total = total + got2[off]
    row = jnp.sum(total, axis=0, keepdims=True)
    mine = jnp.zeros((1, SN_DEV), jnp.float32)
    for g in range(n_group):
        mine = jnp.where(gi == g, row[:, g * SN_DEV : (g + 1) * SN_DEV], mine)
    load_ref[...] = mine


def on_device(n_group, n_dev, state, limit_slot, wall_owner):
    rows = state.size // LANES
    f32 = jnp.float32
    vmem = pl.BlockSpec(memory_space=pltpu.VMEM)
    out, loads = pl.pallas_call(
        functools.partial(kernel, n_group, n_dev, n_dev * CAP),
        out_shape=(
            jax.ShapeDtypeStruct((rows, LANES), f32),
            jax.ShapeDtypeStruct((1, SN_DEV), f32),
        ),
        in_specs=[vmem, vmem, pl.BlockSpec(memory_space=pltpu.SMEM)],
        out_specs=(vmem, vmem),
        scratch_shapes=[
            pltpu.VMEM((640, LANES), f32),
            pltpu.VMEM((640, LANES), f32),
            pltpu.VMEM((rows, LANES), f32),
            pltpu.VMEM((4, 160, LANES), f32),
            pltpu.VMEM((4, 160, LANES), f32),
            pltpu.VMEM((n_dev, 8, LANES), f32),
            pltpu.VMEM((n_dev, 8, LANES), f32),
            pltpu.VMEM((8, LANES), f32),
            pltpu.VMEM((n_group, 8, LANES), f32),
            pltpu.SemaphoreType.DMA((4,)),
            pltpu.SemaphoreType.DMA((4,)),
            pltpu.SemaphoreType.DMA((n_dev,)),
            pltpu.SemaphoreType.DMA((n_dev,)),
            pltpu.SemaphoreType.DMA((n_group,)),
            pltpu.SemaphoreType.DMA((n_group,)),
        ],
        compiler_params=pltpu.CompilerParams(
            collective_id=0, has_side_effects=True, vmem_limit_bytes=32 * 1024 * 1024
        ),
    )(state.reshape(rows, LANES), limit_slot, wall_owner)
    return out.reshape(state.shape), loads.reshape(SN_DEV)


def solution(mesh):
    in_specs = (
        P(None, None, None, None, "group", "dev", None),
        P("group", "dev", None),
        P("group", "dev", None),
    )
    out_specs = (P(None, None, None, None, "group", "dev", None), P(("group", "dev")))
    return jax.shard_map(
        functools.partial(on_device, mesh.shape["group"], mesh.shape["dev"]),
        mesh=mesh, in_specs=in_specs, out_specs=out_specs, check_vma=False,
    )
```

time: 280 us -> 21.5 us (0.08); the launches traced: 274 us -> 21.3 us
  other arithmetic: 142 us -> 0 us
  local copies, waits for them, and re-layouts: 79.4 us -> 3.79 us
  blocking collectives: 38 us -> 0 us
  Pallas kernels: 0 us -> 16.9 us
  starting transfers between devices: 7.75 us -> 0 us
  matrix products: 5.28 us -> 0 us
    unnamed x142 -> x0, other arithmetic: 63.2 us -> none
    unnamed x1 -> x0, blocking collectives: 38 us -> none
    sub x41 -> x0, other arithmetic: 29.7 us -> none  [the longest x29 26.9 us: rusanov(): 0.5 * (left_flux + right_flux) - 0.5 * fastest * (right_state - left_state)]
    another operation x52 -> x0, other arithmetic: 23.6 us -> none  [the longest x49 23.3 us: euler_flux(): return (jnp.stack(flux_rows), wave_speed)]
    unnamed x196 -> x8, local copies, waits for them, and re-layouts: 26 us -> 3.79 us
    pallas_call x0 -> x1, Pallas kernels: none -> 16.9 us  [on_device(): pl.pallas_call(functools.partial(kernel, n_group, n_dev, n_dev * CAP), ou...]
    mul x27 -> x0, other arithmetic: 15.2 us -> none  [the longest x26 14.6 us: rusanov(): 0.5 * fastest * (right_state - left_state)]
    scatter-add x2 -> x0, local copies, waits for them, and re-layouts: 14.8 us -> none  [the longest x1 7.39 us: dg_rate(): volume.at[high_index].add((flux_high - node_flux[high_index]) / weights[3])]
  transfers between devices with their start and end apart: 4 -> 0, of which waited for: 0 -> 0; matrix products, arithmetic and copies ran while one was open for 30% -> 0% of each run, Pallas kernels for 0% -> 0%
where the time goes in v1:
time: 21.5 us; the launch traced here: 21.3 us
  Pallas kernels  16.9 us (79%)
  local copies, waits for them, and re-layouts  3.79 us (18%)
  between operations  0.65 us (3%)
    pallas_call x1, Pallas kernels, on_device(): pl.pallas_call(functools.partial(kernel, n_group, n_dev, n_dev * CAP), ou...  16.9 us
    unnamed x8, local copies, waits for them, and re-layouts  3.79 us

profile of v1, /device:TPU:0, one launch (start us, length us, event | category | flops | bytes accessed | tf_op | source)
XLA Modules:
  0.0 21.3 jit_solution(965438276612323229)
XLA Ops:
  0.6 0.0 copy-start
  0.6 1.1 %copy-done = f32[5,4,4,4,2,2,128]{6,5,4,3,2,1,0:T(2,128)S(1)} copy-done((f32[5,4,4,4,2,2,128]{6,5,4,3,2,1,0:T(2,128)S(1)}, f32[5,4,4,4,2,2,128]{6,5,4,3,2,1,0:T(2,128)}, u32[]{:S(2)}) %copy-start) | copy-done | bytes 655384
  1.7 0.0 copy-start.1
  1.7 0.7 %copy-done.1 = s32[2,2,128]{2,1,0:T(2,128)S(1)} copy-done((s32[2,2,128]{2,1,0:T(2,128)S(1)}, s32[2,2,128]{2,1,0:T(2,128)}, u32[]{:S(2)}) %copy-start.1) | copy-done | bytes 2072
  2.4 0.0 copy-start.2
  2.4 0.7 %copy-done.2 = s32[2,2,2]{2,1,0:T(2,128)S(1)} copy-done((s32[2,2,2]{2,1,0:T(2,128)S(1)}, s32[2,2,2]{2,1,0:T(2,128)}, u32[]{:S(2)}) %copy-start.2) | copy-done | bytes 56
  3.1 16.9 %shard_map.50 = (f32[1280,128]{1,0:T(8,128)S(1)}, f32[1,8]{1,0:T(1,128)S(1)}) custom-call(f32[1280,128]{1,0:T(8,128)S(1)} %bitcast.3, s32[2,2,128]{2,1,0:T(2,128)S(1)} %copy-done.1, s32[2,2,2]{2,1,0:T(2,128)S(1)} %copy-done.2), custom_call_target="tpu_custom_call" | custom-call | tf_op jit(solution)/shard_map/pallas_call | solution.py:488
  20.0 0.8 %copy.7 = f32[5,4,4,4,2,2,128]{6,5,4,3,2,1,0:T(2,128)} copy(f32[5,4,4,4,2,2,128]{6,5,4,3,2,1,0:T(2,128)S(1)} %bitcast.4) | data formatting | bytes 1310720
  20.8 0.5 %copy.8 = f32[8]{0:T(128)} copy(f32[8]{0:T(128)S(1)} %bitcast.5) | data formatting | bytes 64
Async XLA Ops:
  0.6 1.1 %copy-start = (f32[5,4,4,4,2,2,128]{6,5,4,3,2,1,0:T(2,128)S(1)}, f32[5,4,4,4,2,2,128]{6,5,4,3,2,1,0:T(2,128)}, u32[]{:S(2)}) copy-start(f32[5,4,4,4,2,2,128]{6,5,4,3,2,1,0:T(2,128)} %param.3) | copy-start | bytes 1966084
  1.7 0.7 %copy-start.1 = (s32[2,2,128]{2,1,0:T(2,128)S(1)}, s32[2,2,128]{2,1,0:T(2,128)}, u32[]{:S(2)}) copy-start(s32[2,2,128]{2,1,0:T(2,128)} %slot_ref.1) | copy-start | bytes 6148
  2.4 0.7 %copy-start.2 = (s32[2,2,2]{2,1,0:T(2,128)S(1)}, s32[2,2,2]{2,1,0:T(2,128)}, u32[]{:S(2)}) copy-start(s32[2,2,2]{2,1,0:T(2,128)} %owner_ref.1) | copy-start | bytes 100

commit v2 on v1

--- a/solution.py
+++ b/solution.py
@@ -68,6 +68,11 @@
 def combine(ul, fl, sl, ur, fr, sr):
     half = 0.5 * jnp.maximum(sl, sr)
     return [0.5 * (fl[c] + fr[c]) - half * (ur[c] - ul[c]) for c in range(5)]
+
+
+def combine_twice(ul, fl, sl, ur, fr, sr):
+    fastest = jnp.maximum(sl, sr)
+    return [(fl[c] + fr[c]) - fastest * (ur[c] - ul[c]) for c in range(5)]
 
 
 def rusanov(ul, ur, d):
@@ -145,29 +150,6 @@
 
     lax.fori_loop(0, 4, pack, 0)
 
-    pl.semaphore_wait(barrier, n_dev - 1 + n_group - 1)
-
-    halo_copies = []
-    for d in range(2):
-        for side in range(2):
-            step = 1 if side == 1 else -1
-            if d == 0:
-                target = (lax.rem(gi + step + n_group, n_group), di)
-            else:
-                target = (gi, lax.rem(di + step + n_dev, n_dev))
-            slot = 2 * d + side
-            arrive = 2 * d + 1 - side
-            copy = pltpu.make_async_remote_copy(
-                src_ref=send_halo.at[slot],
-                dst_ref=recv_halo.at[arrive],
-                send_sem=hs.at[slot],
-                recv_sem=hr.at[arrive],
-                device_id=target,
-                device_id_type=MESH,
-            )
-            copy.start()
-            halo_copies.append(copy)
-
     wij = [[float(WEIGHTS[i] * WEIGHTS[j]) for j in range(4)] for i in range(4)]
     weight_node = lambda a: jnp.where((a == 0) | (a == 3), float(WEIGHTS[0]), float(WEIGHTS[1]))
 
@@ -193,7 +175,7 @@
                 load = load + (weight_node(i) * weight_node(j)) * both
         return load
 
-    load = lax.fori_loop(0, 16, z_faces, jnp.zeros((8, LANES), jnp.float32))
+    load = lax.fori_loop(0, 16, z_faces, jnp.zeros((8, LANES), jnp.float32), unroll=4)
 
     value = jnp.where(lower, -load, load)
     wall_lane = jnp.where(lower, 0, LANES - 1)
@@ -205,22 +187,46 @@
                 owner = jnp.where(sub == s * 4 + x * 2 + y, owner_ref[x, y, s], owner)
     group_base = (lane // SN_DEV) * (n_dev * SN_DEV) + lax.rem(lane, SN_DEV)
     used = lane < n_group * SN_DEV
-    copies1 = []
     for off in range(n_dev):
         peer = lax.rem(di + off, n_dev)
         match = (owner == group_base + peer * SN_DEV) & used
         part1[off] = jnp.where(match, value, 0.0)
-        if off:
+
+    pl.semaphore_wait(barrier, n_dev - 1 + n_group - 1)
+
+    halo_copies = []
+    for d in range(2):
+        for side in range(2):
+            step = 1 if side == 1 else -1
+            if d == 0:
+                target = (lax.rem(gi + step + n_group, n_group), di)
+            else:
+                target = (gi, lax.rem(di + step + n_dev, n_dev))
+            slot = 2 * d + side
+            arrive = 2 * d + 1 - side
             copy = pltpu.make_async_remote_copy(
-                src_ref=part1.at[off],
-                dst_ref=got1.at[off],
-                send_sem=s1.at[off],
-                recv_sem=r1.at[off],
-                device_id=(gi, peer),
+                src_ref=send_halo.at[slot],
+                dst_ref=recv_halo.at[arrive],
+                send_sem=hs.at[slot],
+                recv_sem=hr.at[arrive],
+                device_id=target,
                 device_id_type=MESH,
             )
             copy.start()
-            copies1.append(copy)
+            halo_copies.append(copy)
+
+    copies1 = []
+    for off in range(1, n_dev):
+        copy = pltpu.make_async_remote_copy(
+            src_ref=part1.at[off],
+            dst_ref=got1.at[off],
+            send_sem=s1.at[off],
+            recv_sem=r1.at[off],
+            device_id=(gi, lax.rem(di + off, n_dev)),
+            device_id_type=MESH,
+        )
+        copy.start()
+        copies1.append(copy)
 
     dt = courant
     vol = [[float(VOLUME[a, b]) for b in range(4)] for a in range(4)]
@@ -239,7 +245,7 @@
                 put(out_ref, node(c, a, j, kp), cols[a][0][c] - dt * rate)
         return carry
 
-    lax.fori_loop(0, 8, x_part, 0)
+    lax.fori_loop(0, 8, x_part, 0, unroll=2)
 
     def y_part(q, carry):
         i, kp = q // 2, q % 2
@@ -251,7 +257,7 @@
                 put(out_ref, index, tile(out_ref, index) - dt * rate)
         return carry
 
-    lax.fori_loop(0, 8, y_part, 0)
+    lax.fori_loop(0, 8, y_part, 0, unroll=2)
 
     def halves(a, b):
         return jnp.where(lower, -dt * vol[a[0]][a[1]], -dt * vol[b[0]][b[1]])
@@ -279,7 +285,7 @@
                 put(out_ref, index, tile(out_ref, index) + rate)
         return carry
 
-    lax.fori_loop(0, 16, z_part, 0)
+    lax.fori_loop(0, 16, z_part, 0, unroll=4)
 
     for copy in copies1:
         copy.wait()
@@ -350,7 +356,7 @@
     kmod = lax.rem(sub, 4)
     k_first, k_last = kmod == 0, kmod == 3
     edge, inner = 1.0 / float(WEIGHTS[0]), 1.0 / float(WEIGHTS[1])
-    sub_dt = courant / SUBSTEPS
+    sub_dt = 0.5 * courant / SUBSTEPS
     wk = jnp.where(k_first | k_last, sub_dt * edge, sub_dt * inner)
     wj = [
         jnp.where(lower, sub_dt * edge, sub_dt * inner),
@@ -389,6 +395,8 @@
             for t in range(8)
         )
 
+        px, py, pz = px + px, py + py, pz + pz
+
         def substep(_, flat):
             u = [[flat[c * 8 + t] for c in range(5)] for t in range(8)]
             prim = [primitives(u[t]) for t in range(8)]
@@ -407,7 +415,7 @@
                 g = [[cut(px, (c * 2 + 0) * 2 + jp) for c in range(5)]]
                 for a in range(3):
                     l, r = a * 2 + jp, (a + 1) * 2 + jp
-                    g.append(combine(u[l], f[l][0], f[l][1], u[r], f[r][0], f[r][1]))
+                    g.append(combine_twice(u[l], f[l][0], f[l][1], u[r], f[r][0], f[r][1]))
                 g.append([cut(px, (c * 2 + 1) * 2 + jp) for c in range(5)])
                 for a in range(4):
                     t = a * 2 + jp
@@ -428,11 +436,11 @@
                     )
                 ra, rb = rolled
                 mix = lambda a, b: [jnp.where(lower, x, y) for x, y in zip(a, b)]
-                ga = combine(
+                ga = combine_twice(
                     u[t0], f[t0][0], f[t0][1],
                     mix(ra[0], rb[0]), mix(ra[1], rb[1]), jnp.where(lower, ra[2], rb[2]),
                 )
-                gb = combine(u[t1], f[t1][0], f[t1][1], rb[0], rb[1], rb[2])
+                gb = combine_twice(u[t1], f[t1][0], f[t1][1], rb[0], rb[1], rb[2])
                 for c in range(5):
                     bound = cut(py, c * 4 + i)
                     high1 = jnp.where(lower, gb[c], bound)
@@ -444,7 +452,7 @@
 
             f = fluxes(2)
             for t in range(8):
-                g = combine(
+                g = combine_twice(
                     u[t], f[t][0], f[t][1],
                     [roll(x, -1) for x in u[t]], [roll(x, -1) for x in f[t][0]], roll(f[t][1], -1),
                 )

time: 21.5 us -> 20.4 us (0.949)
  Pallas kernels: 16.9 us -> 15.7 us
    pallas_call x1, Pallas kernels: 16.9 us -> 15.7 us  [on_device(): pl.pallas_call(functools.partial(kernel, n_group, n_dev, n_dev * CAP), ou...]
where the time goes in v2:
time: 20.4 us; the launch traced here: 20.2 us
  Pallas kernels  15.7 us (77%)
  local copies, waits for them, and re-layouts  3.79 us (19%)
  between operations  0.65 us (3%)
    pallas_call x1, Pallas kernels, on_device(): pl.pallas_call(functools.partial(kernel, n_group, n_dev, n_dev * CAP), ou...  15.7 us
    unnamed x8, local copies, waits for them, and re-layouts  3.79 us

profile of v2, /device:TPU:0, one launch (start us, length us, event | category | flops | bytes accessed | tf_op | source)
XLA Modules:
  0.0 20.2 jit_solution(5364244507749595696)
XLA Ops:
  0.6 0.0 copy-start
  0.6 1.1 %copy-done = f32[5,4,4,4,2,2,128]{6,5,4,3,2,1,0:T(2,128)S(1)} copy-done((f32[5,4,4,4,2,2,128]{6,5,4,3,2,1,0:T(2,128)S(1)}, f32[5,4,4,4,2,2,128]{6,5,4,3,2,1,0:T(2,128)}, u32[]{:S(2)}) %copy-start) | copy-done | bytes 655384
  1.7 0.0 copy-start.1
  1.7 0.7 %copy-done.1 = s32[2,2,128]{2,1,0:T(2,128)S(1)} copy-done((s32[2,2,128]{2,1,0:T(2,128)S(1)}, s32[2,2,128]{2,1,0:T(2,128)}, u32[]{:S(2)}) %copy-start.1) | copy-done | bytes 2072
  2.4 0.0 copy-start.2
  2.4 0.7 %copy-done.2 = s32[2,2,2]{2,1,0:T(2,128)S(1)} copy-done((s32[2,2,2]{2,1,0:T(2,128)S(1)}, s32[2,2,2]{2,1,0:T(2,128)}, u32[]{:S(2)}) %copy-start.2) | copy-done | bytes 56
  3.1 15.7 %shard_map.50 = (f32[1280,128]{1,0:T(8,128)S(1)}, f32[1,8]{1,0:T(1,128)S(1)}) custom-call(f32[1280,128]{1,0:T(8,128)S(1)} %bitcast.3, s32[2,2,128]{2,1,0:T(2,128)S(1)} %copy-done.1, s32[2,2,2]{2,1,0:T(2,128)S(1)} %copy-done.2), custom_call_target="tpu_custom_call" | custom-call | tf_op jit(solution)/shard_map/pallas_call | solution.py:496
  18.8 0.8 %copy.7 = f32[5,4,4,4,2,2,128]{6,5,4,3,2,1,0:T(2,128)} copy(f32[5,4,4,4,2,2,128]{6,5,4,3,2,1,0:T(2,128)S(1)} %bitcast.4) | data formatting | bytes 1310720
  19.7 0.5 %copy.8 = f32[8]{0:T(128)} copy(f32[8]{0:T(128)S(1)} %bitcast.5) | data formatting | bytes 64
Async XLA Ops:
  0.6 1.1 %copy-start = (f32[5,4,4,4,2,2,128]{6,5,4,3,2,1,0:T(2,128)S(1)}, f32[5,4,4,4,2,2,128]{6,5,4,3,2,1,0:T(2,128)}, u32[]{:S(2)}) copy-start(f32[5,4,4,4,2,2,128]{6,5,4,3,2,1,0:T(2,128)} %param.3) | copy-start | bytes 1966084
  1.7 0.7 %copy-start.1 = (s32[2,2,128]{2,1,0:T(2,128)S(1)}, s32[2,2,128]{2,1,0:T(2,128)}, u32[]{:S(2)}) copy-start(s32[2,2,128]{2,1,0:T(2,128)} %slot_ref.1) | copy-start | bytes 6148
  2.4 0.7 %copy-start.2 = (s32[2,2,2]{2,1,0:T(2,128)S(1)}, s32[2,2,2]{2,1,0:T(2,128)}, u32[]{:S(2)}) copy-start(s32[2,2,2]{2,1,0:T(2,128)} %owner_ref.1) | copy-start | bytes 100
